TPU v7x, 32 devices: a whole 2x2x4 slice. The times are simulated.
32 devices in a mesh: parts: 2 (over x), inner: 16 (over z, y, core).
Axes of the slice: x: 2, y: 2, z: 4, core: 2. Of those that a mesh axis runs over, the one named last changes fastest.
Arguments:
- query_in: bfloat16 [4096, 2048], P(('parts', 'inner')), parts along dimension 0, may hold values from -6 to 6
- key_in: bfloat16 [4096, 2048], P(('parts', 'inner')), parts along dimension 0, may hold values from -6 to 6
- value_in: bfloat16 [4096, 2048], P(('parts', 'inner')), parts along dimension 0, may hold values from -6 to 6
- grad_out: bfloat16 [4096, 2048], P(('parts', 'inner')), parts along dimension 0, may hold values from -6 to 6
- filter_raw: float32 [2048, 2048], P('inner'), may hold values from -6 to 6
- decay_rate: float32 [2048], replicated, may hold values from 0.5 to 3
- short_weight: float32 [3, 2048], replicated, may hold values from -3.5 to 3.5
Outputs:
- grad_query: bfloat16 [4096, 2048], P(('parts', 'inner')), parts along dimension 0
- grad_key: bfloat16 [4096, 2048], P(('parts', 'inner')), parts along dimension 0
- grad_value: bfloat16 [4096, 2048], P(('parts', 'inner')), parts along dimension 0
- grad_filter: float32 [4096, 2048], P(('parts', 'inner')), parts along dimension 0
- grad_short: float32 [6, 2048], P('parts'), parts along dimension 0
There are 2 independent parts, one for each index of `parts`. A program takes and returns all parts, laid end to end along the dimension named above; an argument that names none is the same for every part. Nothing has to cross between parts.
All inputs are finite; a program needn't handle non-finite values.
Results may differ from a plain program's by a relative error of at most 0.0085.
Values may be sent and summed in bfloat16 or wider, within the bound.
A program may use at most 128 MiB of HBM per device.

v0:
```python
import functools
import math

import jax
import jax.numpy as jnp
import ml_dtypes
import numpy as np
from jax import lax
from jax.experimental import pallas as pl
from jax.experimental.pallas import tpu as pltpu
from jax.sharding import PartitionSpec as P

HIGHEST = lax.Precision.HIGHEST
MESH = pl.DeviceIdType.MESH
F32 = jnp.float32
BF16 = jnp.bfloat16
THETA = 0.25
LANES = 128
CHUNK = 16


def inner_tables(group, rows):
    length = group * rows
    coarse = np.arange(group)[:, None, None]
    fine = np.arange(rows)[None, :, None]
    token = np.arange(rows)[None, None, :]
    angle = 2.0 * np.pi * token * (coarse + THETA + group * fine) / length
    cos, sin = np.cos(angle), np.sin(angle)
    forward = np.concatenate(
        [np.concatenate([cos, sin], axis=2), np.concatenate([-sin, cos], axis=2)], axis=1
    )
    backward = np.swapaxes(forward, 1, 2) / length
    return forward.astype(ml_dtypes.bfloat16), backward.astype(ml_dtypes.bfloat16)


def turn(value, angle):
    re, im = value
    cos, sin = math.cos(angle), math.sin(angle)
    if abs(sin) < 1e-12:
        return (re, im) if cos > 0 else (-re, -im)
    if abs(cos) < 1e-12:
        return (-im, re) if sin > 0 else (im, -re)
    if abs(abs(cos) - abs(sin)) < 1e-12:
        cs, sn = math.copysign(1, cos), math.copysign(1, sin)
        size = abs(cos)
        real = (re if cs > 0 else -re) - (im if sn > 0 else -im)
        imag = (im if cs > 0 else -im) + (re if sn > 0 else -re)
        return (real * size, imag * size)
    return (re * cos - im * sin, im * cos + re * sin)


def small_transform(values, sign):
    count = len(values)
    if count == 1:
        return values
    even = small_transform(values[0::2], sign)
    odd = small_transform(values[1::2], sign)
    half = count // 2
    low, high = [], []
    for k in range(half):
        a = even[k]
        b = turn(odd[k], sign * 2.0 * math.pi * k / count)
        low.append((a[0] + b[0], a[1] + b[1]))
        high.append((a[0] - b[0], a[1] - b[1]))
    return low + high


def outer_forward(group, source, target, row0, columns):
    rows = source.shape[1]

    def chunk(i, carry):
        at = pl.ds(pl.multiple_of(i * CHUNK, CHUNK), CHUNK)
        values = []
        for a in range(group):
            x = source[a, at, :].astype(F32)
            angle = -2.0 * math.pi * a * THETA / group
            values.append((x * math.cos(angle), x * math.sin(angle)))
        for k, (re, im) in enumerate(small_transform(values, -1.0)):
            target[k, at, columns] = re.astype(BF16)
            later = pl.ds(pl.multiple_of(rows + i * CHUNK, CHUNK), CHUNK)
            target[k, later, columns] = im.astype(BF16)
        return carry

    lax.fori_loop(0, rows // CHUNK, chunk, 0)


def outer_backward(group, source, columns, target):
    rows = target.shape[1]

    def chunk(i, carry):
        at = pl.ds(pl.multiple_of(i * CHUNK, CHUNK), CHUNK)
        later = pl.ds(pl.multiple_of(rows + i * CHUNK, CHUNK), CHUNK)
        values = [(source[k, at, columns], source[k, later, columns]) for k in range(group)]
        for a, (re, im) in enumerate(small_transform(values, 1.0)):
            angle = 2.0 * math.pi * a * THETA / group
            target[a, at, :] = (re * math.cos(angle) - im * math.sin(angle)).astype(BF16)
        return carry

    lax.fori_loop(0, rows // CHUNK, chunk, 0)


def kernel(
    group,
    query, key, value, grad, filt, decay, taps, table_f_hbm, table_b_hbm,
    out_query, out_key, out_value, out_filter, out_short,
    table_f, table_b, stage, recv, shaped, lines, spectra, waves,
    back, home, shaped_grad, rim_value, rim_grad, tap_part, tap_recv, tap_sum, tap_all,
    table_sem, send_sem, recv_sem, back_send, back_recv,
    rim_send, rim_recv, tap_send, tap_rsem, sum_send, sum_recv,
):
    rows = query.shape[0]
    length = rows * group
    scale = 1.0 / math.sqrt(length)
    me = lax.axis_index("inner")
    right, left = lax.rem(me + 1, group), lax.rem(me + group - 1, group)

    load_f = pltpu.make_async_copy(table_f_hbm, table_f, table_sem.at[0])
    load_b = pltpu.make_async_copy(table_b_hbm, table_b, table_sem.at[1])
    load_f.start()
    load_b.start()

    barrier = pltpu.get_barrier_semaphore()

    def greet(s, carry):
        pl.semaphore_signal(
            barrier, inc=1, device_id={"inner": lax.rem(me + s, group)}, device_id_type=MESH
        )
        return carry

    lax.fori_loop(1, group, greet, 0)

    def cols(p):
        return pl.ds(pl.multiple_of(p * LANES, LANES), LANES)

    def remote(src, dst, send, receive, device):
        return pltpu.make_async_remote_copy(
            src_ref=src, dst_ref=dst, send_sem=send, recv_sem=receive,
            device_id={"inner": device}, device_id_type=MESH,
        )

    def forward_copy(kind, s):
        peer = lax.rem(me + s, group)
        return remote(
            stage.at[kind, peer], recv.at[kind, me],
            send_sem.at[kind, s], recv_sem.at[kind, s], peer,
        )

    def back_copy(kind, s):
        peer = lax.rem(me + s, group)
        return remote(
            back.at[kind, peer], home.at[kind, me],
            back_send.at[kind, s], back_recv.at[kind, s], peer,
        )

    def envelope(p):
        line = lax.broadcasted_iota(jnp.int32, (rows, LANES), 0) + me * rows
        return jnp.exp(-decay[:, cols(p)] * line.astype(F32) / length) * scale

    def make_gated(p):
        return (query[:, cols(p)].astype(F32) * grad[:, cols(p)].astype(F32)).astype(BF16)

    def extended(p):
        rim = rim_value[:, cols(p)].astype(F32)
        rim = jnp.where(me == 0, jnp.zeros_like(rim), rim)
        ext = jnp.concatenate([rim, value[:, cols(p)].astype(F32)], axis=0)
        return ext[CHUNK:], ext[CHUNK - 1 : CHUNK - 1 + rows], ext[CHUNK - 2 : CHUNK - 2 + rows]

    def make_mixed(p):
        now, one, two = extended(p)
        weight = taps[:, cols(p)]
        low = (weight[0:1] * now + weight[1:2] * one + weight[2:3] * two).astype(BF16)
        shaped[p] = low
        return (key[:, cols(p)].astype(F32) * low.astype(F32)).astype(BF16)

    def make_lagged(p):
        return (filt[:, cols(p)] * envelope(p)).astype(BF16)

    def fill_own(kind, make):
        recv[kind, me] = make(me)

    def send_all(kind, make):
        def step(s, carry):
            peer = lax.rem(me + s, group)
            stage[kind, peer] = make(peer)
            forward_copy(kind, s).start()
            return carry

        lax.fori_loop(1, group, step, 0)

    fill_own(0, make_gated)
    fill_own(2, make_lagged)
    pl.semaphore_wait(barrier, group - 1)

    rim_copy = remote(
        value.at[pl.ds(rows - CHUNK, CHUNK), :], rim_value, rim_send.at[0], rim_recv.at[0], right
    )
    rim_copy.start()
    send_all(0, make_gated)
    rim_copy.wait_recv()
    send_all(1, make_mixed)
    fill_own(1, make_mixed)
    send_all(2, make_lagged)

    def await_all(copy, kind):
        def step(s, carry):
            copy(kind, s).wait_recv()
            return carry

        lax.fori_loop(1, group, step, 0)

    low, high = pl.ds(0, LANES), pl.ds(LANES, LANES)
    await_all(forward_copy, 0)
    outer_forward(group, recv.at[0], lines, 0, low)
    await_all(forward_copy, 1)
    outer_forward(group, recv.at[1], lines, 0, high)
    load_f.wait()
    load_b.wait()

    def lag_step(k, carry):
        both = jnp.dot(table_f[k], lines[k], preferred_element_type=F32)
        spectra[k] = both
        g_re, g_im = both[:rows, :LANES], both[rows:, :LANES]
        m_re, m_im = both[:rows, LANES:], both[rows:, LANES:]
        product = jnp.concatenate(
            [g_re * m_re + g_im * m_im, g_im * m_re - g_re * m_im], axis=0
        ).astype(BF16)
        waves[k, :, low] = jnp.dot(table_b[k], product, preferred_element_type=F32)
        return carry

    lax.fori_loop(0, group, lag_step, 0)
    outer_backward(group, waves, low, back.at[2])

    def return_all(kind):
        def step(s, carry):
            back_copy(kind, s).start()
            return carry

        lax.fori_loop(1, group, step, 0)

    return_all(2)

    await_all(forward_copy, 2)
    outer_forward(group, recv.at[2], lines, 0, low)

    def conv_step(k, carry):
        own = jnp.dot(table_f[k], lines[k, :, low], preferred_element_type=F32)
        l_re, l_im = own[:rows], own[rows:]
        both = spectra[k]
        g_re, g_im = both[:rows, :LANES], both[rows:, :LANES]
        m_re, m_im = both[:rows, LANES:], both[rows:, LANES:]
        grad_part = jnp.concatenate(
            [l_re * g_re + l_im * g_im, l_re * g_im - l_im * g_re], axis=0
        ).astype(BF16)
        conv_part = jnp.concatenate(
            [l_re * m_re - l_im * m_im, l_re * m_im + l_im * m_re], axis=0
        ).astype(BF16)
        product = jnp.concatenate([grad_part, conv_part], axis=1)
        waves[k] = jnp.dot(table_b[k], product, preferred_element_type=F32)
        return carry

    lax.fori_loop(0, group, conv_step, 0)
    outer_backward(group, waves, low, back.at[0])
    return_all(0)
    outer_backward(group, waves, high, back.at[1])
    return_all(1)

    def keep_own(kind):
        home[kind, me] = back[kind, me]

    keep_own(2)
    keep_own(0)
    keep_own(1)

    await_all(back_copy, 2)

    def filter_step(p, carry):
        out_filter[:, cols(p)] = home[2, p].astype(F32) * envelope(p)
        return carry

    lax.fori_loop(0, group, filter_step, 0)

    await_all(back_copy, 0)

    def grad_step(p, carry):
        mixed_grad = home[0, p].astype(F32)
        out_key[:, cols(p)] = (mixed_grad * shaped[p].astype(F32)).astype(BF16)
        low_grad = (mixed_grad * key[:, cols(p)].astype(F32)).astype(BF16)
        shaped_grad[p] = low_grad
        line = low_grad.astype(F32)
        now, one, two = extended(p)
        sums = [jnp.sum(line * x, axis=0, keepdims=True) for x in (now, one, two)]
        tap_part[p] = jnp.concatenate(sums + [jnp.zeros((5, LANES), F32)], axis=0)
        return carry

    lax.fori_loop(0, group, grad_step, 0)
    rim_back = remote(
        shaped_grad.at[:, pl.ds(0, CHUNK), :], rim_grad, rim_send.at[1], rim_recv.at[1], left
    )
    rim_back.start()

    def tap_copy(s):
        peer = lax.rem(me + s, group)
        return remote(tap_part.at[peer], tap_recv.at[me], tap_send.at[s], tap_rsem.at[s], peer)

    def sum_copy(s):
        peer = lax.rem(me + s, group)
        return remote(tap_sum, tap_all.at[me], sum_send.at[s], sum_recv.at[s], peer)

    def loop(body):
        def step(s, carry):
            body(s)
            return carry

        lax.fori_loop(1, group, step, 0)

    loop(lambda s: tap_copy(s).start())
    tap_recv[me] = tap_part[me]
    rim_back.wait_recv()

    def value_step(p, carry):
        rim = rim_grad[p].astype(F32)
        rim = jnp.where(me == group - 1, jnp.zeros_like(rim), rim)
        ext = jnp.concatenate([shaped_grad[p].astype(F32), rim], axis=0)
        weight = taps[:, cols(p)]
        total = weight[0:1] * ext[:rows] + weight[1:2] * ext[1 : rows + 1]
        out_value[:, cols(p)] = (total + weight[2:3] * ext[2 : rows + 2]).astype(BF16)
        return carry

    lax.fori_loop(0, group, value_step, 0)
    loop(lambda s: tap_copy(s).wait_recv())
    tap_sum[...] = jnp.sum(tap_recv[...], axis=0) * scale
    loop(lambda s: sum_copy(s).start())
    tap_all[me] = tap_sum[...]

    await_all(back_copy, 1)

    def query_step(p, carry):
        conv = home[1, p].astype(F32)
        out_query[:, cols(p)] = (grad[:, cols(p)].astype(F32) * conv).astype(BF16)
        return carry

    lax.fori_loop(0, group, query_step, 0)
    loop(lambda s: sum_copy(s).wait_recv())
    for p in range(group):
        out_short[:, p * LANES : (p + 1) * LANES] = tap_all[p][0:3]

    def drain(s):
        for kind in range(3):
            forward_copy(kind, s).wait_send()
            back_copy(kind, s).wait_send()
        tap_copy(s).wait_send()
        sum_copy(s).wait_send()

    loop(drain)
    rim_copy.wait_send()
    rim_back.wait_send()


def fused(group, query_in, key_in, value_in, grad_out, filter_raw, decay_rate, short_weight):
    rows, channels = query_in.shape
    table_f, table_b = inner_tables(group, rows)
    vmem = pl.BlockSpec(memory_space=pltpu.VMEM)
    blocks = (group, rows, LANES)
    dma = pltpu.SemaphoreType.DMA
    return pl.pallas_call(
        functools.partial(kernel, group),
        out_shape=(
            jax.ShapeDtypeStruct((rows, channels), BF16),
            jax.ShapeDtypeStruct((rows, channels), BF16),
            jax.ShapeDtypeStruct((rows, channels), BF16),
            jax.ShapeDtypeStruct((rows, channels), F32),
            jax.ShapeDtypeStruct((3, channels), F32),
        ),
        in_specs=[vmem] * 7 + [pl.BlockSpec(memory_space=pl.ANY)] * 2,
        out_specs=(vmem,) * 5,
        scratch_shapes=[
            pltpu.VMEM(table_f.shape, BF16),
            pltpu.VMEM(table_b.shape, BF16),
            pltpu.VMEM((3,) + blocks, BF16),
            pltpu.VMEM((3,) + blocks, BF16),
            pltpu.VMEM(blocks, BF16),
            pltpu.VMEM((group, 2 * rows, 2 * LANES), BF16),
            pltpu.VMEM((group, 2 * rows, 2 * LANES), F32),
            pltpu.VMEM((group, 2 * rows, 2 * LANES), F32),
            pltpu.VMEM((3,) + blocks, BF16),
            pltpu.VMEM((3,) + blocks, BF16),
            pltpu.VMEM(blocks, BF16),
            pltpu.VMEM((CHUNK, channels), BF16),
            pltpu.VMEM((group, CHUNK, LANES), BF16),
            pltpu.VMEM((group, 8, LANES), F32),
            pltpu.VMEM((group, 8, LANES), F32),
            pltpu.VMEM((8, LANES), F32),
            pltpu.VMEM((group, 8, LANES), F32),
            dma((2,)),
            dma((3, group)),
            dma((3, group)),
            dma((3, group)),
            dma((3, group)),
            dma((2,)),
            dma((2,)),
            dma((group,)),
            dma((group,)),
            dma((group,)),
            dma((group,)),
        ],
        compiler_params=pltpu.CompilerParams(
            collective_id=0, has_side_effects=True, vmem_limit_bytes=56 * 2**20
        ),
    )(
        query_in, key_in, value_in, grad_out, filter_raw,
        decay_rate.reshape(1, channels), short_weight,
        jnp.asarray(table_f), jnp.asarray(table_b),
    )


def shifted(block, axis, distance):
    devices = range(lax.axis_size(axis))
    route = [(i - distance, i) for i in devices if i - distance in devices]
    return lax.ppermute(block, axis, route)


def dft_tables(length):
    index_line = jnp.arange(length, dtype=jnp.int32)
    phase_int = index_line[:, None] * index_line[None, :] % length
    angles = phase_int.astype(jnp.float32) * (-2.0 * math.pi / length)
    return (jnp.cos(angles), jnp.sin(angles))


def twist_tables(outer_size, inner_size, length):
    outer_line = jnp.arange(outer_size, dtype=jnp.int32)
    inner_line = jnp.arange(inner_size, dtype=jnp.int32)
    phase_int = outer_line[:, None] * inner_line[None, :] % length
    angles = phase_int.astype(jnp.float32) * (-2.0 * math.pi / length)
    return (jnp.cos(angles), jnp.sin(angles))


def right_multiply(values, table):
    return jnp.einsum("ckn,nm->ckm", values, table, precision=HIGHEST)


def forward_transform(signal, tables):
    cos_outer, sin_outer, cos_inner, sin_inner, twist_cos, twist_sin = tables
    channels = signal.shape[0]
    half_rows = cos_outer.shape[0] // 2
    blocks = signal.reshape(channels, half_rows, cos_inner.shape[0])
    first_re = jnp.einsum("kn,cna->cka", cos_outer[:, :half_rows], blocks, precision=HIGHEST)
    first_im = jnp.einsum("kn,cna->cka", sin_outer[:, :half_rows], blocks, precision=HIGHEST)
    turned_re = first_re * twist_cos - first_im * twist_sin
    turned_im = first_re * twist_sin + first_im * twist_cos
    spec_re = right_multiply(turned_re, cos_inner) - right_multiply(turned_im, sin_inner)
    spec_im = right_multiply(turned_re, sin_inner) + right_multiply(turned_im, cos_inner)
    return (spec_re, spec_im)


def inverse_transform(spec_re, spec_im, tables):
    cos_outer, sin_outer, cos_inner, sin_inner, twist_cos, twist_sin = tables
    channels = spec_re.shape[0]
    half_rows = cos_outer.shape[0] // 2
    back_re = right_multiply(spec_re, cos_inner) + right_multiply(spec_im, sin_inner)
    back_im = right_multiply(spec_im, cos_inner) - right_multiply(spec_re, sin_inner)
    turned_re = back_re * twist_cos + back_im * twist_sin
    turned_im = back_im * twist_cos - back_re * twist_sin
    signal = jnp.einsum("nk,cka->cna", cos_outer[:half_rows], turned_re, precision=HIGHEST)
    signal = signal + jnp.einsum("nk,cka->cna", sin_outer[:half_rows], turned_im, precision=HIGHEST)
    scaled = signal * (1.0 / (cos_outer.shape[0] * cos_inner.shape[0]))
    return scaled.reshape(channels, -1)


def per_device(query_in, key_in, value_in, grad_out, filter_raw, decay_rate, short_weight):
    local_rows = query_in.shape[0]
    group_size = lax.axis_size("inner")
    seq_length = local_rows * group_size
    scale_factor = 1.0 / math.sqrt(seq_length)
    first_row = lax.axis_index("inner") * local_rows
    position = (first_row + jnp.arange(local_rows, dtype=jnp.int32)).astype(jnp.float32)
    envelope = jnp.exp(-decay_rate[None, :] * position[:, None] / seq_length) * scale_factor
    rim_rows = shifted(value_in[local_rows - 2 :], "inner", 1)
    extended = jnp.concatenate([rim_rows, value_in], axis=0).astype(jnp.float32)
    value_now = extended[2:]
    value_one = extended[1:-1]
    value_two = extended[:-2]
    shaped = (
        short_weight[0] * value_now + short_weight[1] * value_one + short_weight[2] * value_two
    ).astype(jnp.bfloat16)
    mixed = (key_in.astype(jnp.float32) * shaped.astype(jnp.float32)).astype(jnp.bfloat16)
    gated = (query_in.astype(jnp.float32) * grad_out.astype(jnp.float32)).astype(jnp.bfloat16)
    lagged = filter_raw * envelope
    mixed_half, gated_half = (
        lax.all_to_all(mixed.T, "inner", split_axis=0, concat_axis=1, tiled=True),
        lax.all_to_all(gated.T, "inner", split_axis=0, concat_axis=1, tiled=True),
    )
    filter_cols = lax.all_to_all(lagged.T, "inner", split_axis=0, concat_axis=1, tiled=True)
    mixed_cols = mixed_half.astype(jnp.float32)
    gated_cols = gated_half.astype(jnp.float32)
    fft_length = 2 * seq_length
    exponent = fft_length.bit_length() - 1
    inner_size = 2 ** (exponent // 2)
    outer_size = fft_length // inner_size
    cos_outer, sin_outer = dft_tables(outer_size)
    cos_inner, sin_inner = dft_tables(inner_size)
    twist_cos, twist_sin = twist_tables(outer_size, inner_size, fft_length)
    tables = (cos_outer, sin_outer, cos_inner, sin_inner, twist_cos, twist_sin)
    mix_re, mix_im = forward_transform(mixed_cols, tables)
    gate_re, gate_im = forward_transform(gated_cols, tables)
    filt_re, filt_im = forward_transform(filter_cols, tables)
    conv_cols = inverse_transform(
        filt_re * mix_re - filt_im * mix_im, filt_re * mix_im + filt_im * mix_re, tables
    )
    grad_cols = inverse_transform(
        filt_re * gate_re + filt_im * gate_im, filt_re * gate_im - filt_im * gate_re, tables
    )
    lag_cols = inverse_transform(
        gate_re * mix_re + gate_im * mix_im, gate_im * mix_re - gate_re * mix_im, tables
    )
    conv_low = conv_cols.astype(jnp.bfloat16)
    grad_low = grad_cols.astype(jnp.bfloat16)
    conv_rows, grad_rows = (
        lax.all_to_all(conv_low, "inner", split_axis=1, concat_axis=0, tiled=True),
        lax.all_to_all(grad_low, "inner", split_axis=1, concat_axis=0, tiled=True),
    )
    lag_rows = lax.all_to_all(lag_cols, "inner", split_axis=1, concat_axis=0, tiled=True)
    conv = conv_rows.T.astype(jnp.float32)
    grad_mixed = grad_rows.T.astype(jnp.float32)
    grad_lag = lag_rows.T
    grad_query = (grad_out.astype(jnp.float32) * conv).astype(jnp.bfloat16)
    grad_key = (grad_mixed * shaped.astype(jnp.float32)).astype(jnp.bfloat16)
    grad_shaped = (grad_mixed * key_in.astype(jnp.float32)).astype(jnp.bfloat16)
    next_rows = shifted(grad_shaped[:2], "inner", -1)
    grad_ext = jnp.concatenate([grad_shaped, next_rows], axis=0).astype(jnp.float32)
    grad_now = grad_ext[:local_rows]
    grad_one = grad_ext[1 : local_rows + 1]
    grad_two = grad_ext[2:]
    grad_value = (
        short_weight[0] * grad_now + short_weight[1] * grad_one + short_weight[2] * grad_two
    ).astype(jnp.bfloat16)
    partial_taps = jnp.stack(
        [
            jnp.sum(grad_now * value_now, axis=0),
            jnp.sum(grad_now * value_one, axis=0),
            jnp.sum(grad_now * value_two, axis=0),
        ]
    )
    grad_short = lax.psum(partial_taps, "inner") * scale_factor
    grad_filter = grad_lag * envelope
    return (grad_query, grad_key, grad_value, grad_filter, grad_short)


def dispatch(*arrays):
    rows, channels = arrays[0].shape
    group = lax.axis_size("inner")
    if rows == LANES and group == 16 and channels == group * LANES:
        return fused(group, *arrays)
    return per_device(*arrays)


def solution(mesh):
    in_specs = (
        P(("parts", "inner"), None),
        P(("parts", "inner"), None),
        P(("parts", "inner"), None),
        P(("parts", "inner"), None),
        P("inner", None),
        P(),
        P(),
    )
    out_specs = (
        P(("parts", "inner"), None),
        P(("parts", "inner"), None),
        P(("parts", "inner"), None),
        P(("parts", "inner"), None),
        P("parts", None),
    )
    return jax.shard_map(
        dispatch, mesh=mesh, in_specs=in_specs, out_specs=out_specs, check_vma=False
    )
```

profile of v0, /device:TPU:0, one launch (start us, length us, event | category | flops | bytes accessed | tf_op | source)
XLA Modules:
  0.0 97.8 jit_solution(9363375700402209366)
XLA Ops:
  0.6 90.9 %shard_map.128 = (bf16[128,2048]{1,0:T(8,128)(2,1)}, bf16[128,2048]{1,0:T(8,128)(2,1)}, bf16[128,2048]{1,0:T(8,128)(2,1)}, f32[128,2048]{1,0:T(8,128)}, f32[3,2048]{1,0:T(4,128)}) custom-call(bf16[128,2048]{1,0:T(8,128)(2,1)} %query.1, bf16[128,2048]{1,0:T(8,128)(2,1)} %key.1, bf16[128,2048]{1,0:T(8,128)(2,1)} %value.1, bf16[128,2048]{1,0:T(8,128)(2,1)} %grad.1, ...), custom_call_target="tpu_custom_call" | custom-call | tf_op jit(solution)/shard_map/pallas_call | solution.py:365
  91.5 0.0 copy-start.1
  91.5 0.0 copy-start
  91.5 2.0 %copy.19 = bf16[128,2048]{1,0:T(8,128)(2,1)} copy(bf16[128,2048]{1,0:T(8,128)(2,1)} %get-tuple-element.10) | data formatting | bytes 1048576
  93.5 0.0 copy-start.2
  93.5 1.9 %copy.20 = bf16[128,2048]{1,0:T(8,128)(2,1)} copy(bf16[128,2048]{1,0:T(8,128)(2,1)} %get-tuple-element.11) | data formatting | bytes 1048576
  95.4 0.0 copy-done.1
  95.4 0.8 copy.21
  96.2 0.0 copy-done
  96.2 1.0 copy.22
  97.2 0.0 copy-done.2
  97.2 0.6 copy.23
Async XLA Ops:
  91.5 3.9 %copy-start.1 = (bf16[128,2048]{1,0:T(8,128)(2,1)S(1)}, bf16[128,2048]{1,0:T(8,128)(2,1)}, u32[]{:S(2)}) copy-start(bf16[128,2048]{1,0:T(8,128)(2,1)} %get-tuple-element.12) | copy-start | bytes 1572868
  91.5 4.7 %copy-start = (f32[128,2048]{1,0:T(8,128)S(1)}, f32[128,2048]{1,0:T(8,128)}, u32[]{:S(2)}) copy-start(f32[128,2048]{1,0:T(8,128)} %get-tuple-element.13) | copy-start | bytes 3145732
  93.5 3.7 %copy-start.2 = (f32[3,2048]{1,0:T(4,128)S(1)}, f32[3,2048]{1,0:T(4,128)}, u32[]{:S(2)}) copy-start(f32[3,2048]{1,0:T(4,128)} %get-tuple-element.14) | copy-start | bytes 73732
where the time goes:
time: 98 us; the launch traced here: 97.8 us
  Pallas kernels  90.9 us (93%)
  local copies, waits for them, and re-layouts  6.27 us (6%)
    pallas_call x1, Pallas kernels, fused(): pl.pallas_call(functools.partial(kernel, group), out_shape=(jax.ShapeDtyp...  90.9 us
    unnamed x11, local copies, waits for them, and re-layouts  6.27 us

commit v1 on v0

--- a/solution.py
+++ b/solution.py
@@ -17,6 +17,7 @@
 THETA = 0.25
 LANES = 128
 CHUNK = 16
+CUT_ONE, CUT_TWO = 8, 13
 
 
 def inner_tables(group, rows):
@@ -106,7 +107,7 @@
     table_f, table_b, stage, recv, shaped, lines, spectra, waves,
     back, home, shaped_grad, rim_value, rim_grad, tap_part, tap_recv, tap_sum, tap_all,
     table_sem, send_sem, recv_sem, back_send, back_recv,
-    rim_send, rim_recv, tap_send, tap_rsem, sum_send, sum_recv,
+    rim_send, rim_recv, tap_send, tap_rsem, sum_send, sum_recv, twin_send, twin_recv,
 ):
     rows = query.shape[0]
     length = rows * group
@@ -128,6 +129,8 @@
         return carry
 
     lax.fori_loop(1, group, greet, 0)
+    part = lax.axis_index("parts")
+    pl.semaphore_signal(barrier, inc=1, device_id={"parts": 1 - part}, device_id_type=MESH)
 
     def cols(p):
         return pl.ds(pl.multiple_of(p * LANES, LANES), LANES)
@@ -138,15 +141,26 @@
             device_id={"inner": device}, device_id_type=MESH,
         )
 
+    def partner(s):
+        distance = lax.rem(s, 2) * (group // 2) + s // 2
+        peer = 0
+        for bit in range(group.bit_length() - 1):
+            place = 2**bit
+            peer += place * lax.rem(me // place + distance // place, 2)
+        return peer
+
+    def ours(s):
+        return lax.rem(s // 2, 2) == part
+
     def forward_copy(kind, s):
-        peer = lax.rem(me + s, group)
+        peer = partner(s)
         return remote(
             stage.at[kind, peer], recv.at[kind, me],
             send_sem.at[kind, s], recv_sem.at[kind, s], peer,
         )
 
     def back_copy(kind, s):
-        peer = lax.rem(me + s, group)
+        peer = partner(s)
         return remote(
             back.at[kind, peer], home.at[kind, me],
             back_send.at[kind, s], back_recv.at[kind, s], peer,
@@ -180,7 +194,7 @@
 
     def send_all(kind, make):
         def step(s, carry):
-            peer = lax.rem(me + s, group)
+            peer = partner(s)
             stage[kind, peer] = make(peer)
             forward_copy(kind, s).start()
             return carry
@@ -189,7 +203,7 @@
 
     fill_own(0, make_gated)
     fill_own(2, make_lagged)
-    pl.semaphore_wait(barrier, group - 1)
+    pl.semaphore_wait(barrier, group)
 
     rim_copy = remote(
         value.at[pl.ds(rows - CHUNK, CHUNK), :], rim_value, rim_send.at[0], rim_recv.at[0], right
@@ -199,7 +213,43 @@
     rim_copy.wait_recv()
     send_all(1, make_mixed)
     fill_own(1, make_mixed)
-    send_all(2, make_lagged)
+
+    def send_filter(s, carry):
+        @pl.when(ours(s))
+        def _():
+            peer = partner(s)
+            stage[2, peer] = make_lagged(peer)
+            forward_copy(2, s).start()
+
+        return carry
+
+    lax.fori_loop(1, group, send_filter, 0)
+
+    def twin_copy(source):
+        return pltpu.make_async_remote_copy(
+            src_ref=recv.at[2, source], dst_ref=recv.at[2, source],
+            send_sem=twin_send.at[source], recv_sem=twin_recv.at[source],
+            device_id={"parts": 1 - part}, device_id_type=MESH,
+        )
+
+    def pass_on(s, carry):
+        source = partner(s)
+
+        @pl.when(ours(s))
+        def _():
+            forward_copy(2, s).wait_recv()
+            twin_copy(source).start()
+
+        return carry
+
+    def await_twin(s, carry):
+        source = partner(s)
+
+        @pl.when(jnp.logical_not(ours(s)))
+        def _():
+            twin_copy(source).wait_recv()
+
+        return carry
 
     def await_all(copy, kind):
         def step(s, carry):
@@ -227,19 +277,20 @@
         waves[k, :, low] = jnp.dot(table_b[k], product, preferred_element_type=F32)
         return carry
 
-    lax.fori_loop(0, group, lag_step, 0)
+    lax.fori_loop(0, group, lag_step, 0, unroll=4)
+    lax.fori_loop(1, group, pass_on, 0)
     outer_backward(group, waves, low, back.at[2])
 
-    def return_all(kind):
+    def return_all(kind, first=1, last=group):
         def step(s, carry):
             back_copy(kind, s).start()
             return carry
 
-        lax.fori_loop(1, group, step, 0)
+        lax.fori_loop(first, last, step, 0)
 
     return_all(2)
 
-    await_all(forward_copy, 2)
+    lax.fori_loop(1, group, await_twin, 0)
     outer_forward(group, recv.at[2], lines, 0, low)
 
     def conv_step(k, carry):
@@ -258,11 +309,11 @@
         waves[k] = jnp.dot(table_b[k], product, preferred_element_type=F32)
         return carry
 
-    lax.fori_loop(0, group, conv_step, 0)
+    lax.fori_loop(0, group, conv_step, 0, unroll=4)
     outer_backward(group, waves, low, back.at[0])
     return_all(0)
     outer_backward(group, waves, high, back.at[1])
-    return_all(1)
+    return_all(1, 1, CUT_ONE)
 
     def keep_own(kind):
         home[kind, me] = back[kind, me]
@@ -299,11 +350,11 @@
     rim_back.start()
 
     def tap_copy(s):
-        peer = lax.rem(me + s, group)
+        peer = partner(s)
         return remote(tap_part.at[peer], tap_recv.at[me], tap_send.at[s], tap_rsem.at[s], peer)
 
     def sum_copy(s):
-        peer = lax.rem(me + s, group)
+        peer = partner(s)
         return remote(tap_sum, tap_all.at[me], sum_send.at[s], sum_recv.at[s], peer)
 
     def loop(body):
@@ -314,8 +365,8 @@
         lax.fori_loop(1, group, step, 0)
 
     loop(lambda s: tap_copy(s).start())
+    return_all(1, CUT_ONE, CUT_TWO)
     tap_recv[me] = tap_part[me]
-    rim_back.wait_recv()
 
     def value_step(p, carry):
         rim = rim_grad[p].astype(F32)
@@ -326,11 +377,13 @@
         out_value[:, cols(p)] = (total + weight[2:3] * ext[2 : rows + 2]).astype(BF16)
         return carry
 
-    lax.fori_loop(0, group, value_step, 0)
     loop(lambda s: tap_copy(s).wait_recv())
     tap_sum[...] = jnp.sum(tap_recv[...], axis=0) * scale
     loop(lambda s: sum_copy(s).start())
+    return_all(1, CUT_TWO, group)
     tap_all[me] = tap_sum[...]
+    rim_back.wait_recv()
+    lax.fori_loop(0, group, value_step, 0)
 
     await_all(back_copy, 1)
 
@@ -345,15 +398,45 @@
         out_short[:, p * LANES : (p + 1) * LANES] = tap_all[p][0:3]
 
     def drain(s):
+        for kind in range(2):
+            forward_copy(kind, s).wait_send()
         for kind in range(3):
-            forward_copy(kind, s).wait_send()
             back_copy(kind, s).wait_send()
+
+        @pl.when(ours(s))
+        def _():
+            forward_copy(2, s).wait_send()
+            twin_copy(partner(s)).wait_send()
+
         tap_copy(s).wait_send()
         sum_copy(s).wait_send()
 
     loop(drain)
     rim_copy.wait_send()
     rim_back.wait_send()
+
+
+def deliver(results):
+    count = len(results)
+    steps = 4
+
+    def body(*refs):
+        for source, target in zip(refs[:count], refs[count:]):
+            target[...] = source[...]
+
+    def place(x):
+        if x.shape[0] % (steps * CHUNK):
+            return pl.BlockSpec(x.shape, lambda i: (0, 0))
+        return pl.BlockSpec((x.shape[0] // steps, x.shape[1]), lambda i: (i, 0))
+
+    places = [place(x) for x in results]
+    return pl.pallas_call(
+        body,
+        grid=(steps,),
+        out_shape=tuple(jax.ShapeDtypeStruct(x.shape, x.dtype) for x in results),
+        in_specs=places,
+        out_specs=tuple(places),
+    )(*results)
 
 
 def fused(group, query_in, key_in, value_in, grad_out, filter_raw, decay_rate, short_weight):
@@ -362,7 +445,7 @@
     vmem = pl.BlockSpec(memory_space=pltpu.VMEM)
     blocks = (group, rows, LANES)
     dma = pltpu.SemaphoreType.DMA
-    return pl.pallas_call(
+    results = pl.pallas_call(
         functools.partial(kernel, group),
         out_shape=(
             jax.ShapeDtypeStruct((rows, channels), BF16),
@@ -402,6 +485,8 @@
             dma((group,)),
             dma((group,)),
             dma((group,)),
+            dma((group,)),
+            dma((group,)),
         ],
         compiler_params=pltpu.CompilerParams(
             collective_id=0, has_side_effects=True, vmem_limit_bytes=56 * 2**20
@@ -411,6 +496,7 @@
         decay_rate.reshape(1, channels), short_weight,
         jnp.asarray(table_f), jnp.asarray(table_b),
     )
+    return deliver(results)
 
 
 def shifted(block, axis, distance):
@@ -548,7 +634,8 @@
 def dispatch(*arrays):
     rows, channels = arrays[0].shape
     group = lax.axis_size("inner")
-    if rows == LANES and group == 16 and channels == group * LANES:
+    shape_fits = rows == LANES and group == 16 and channels == group * LANES
+    if shape_fits and lax.axis_size("parts") == 2:
         return fused(group, *arrays)
     return per_device(*arrays)
 

time: 98 us -> 88.3 us (0.901)
  local copies, waits for them, and re-layouts: 6.27 us -> 0 us
  Pallas kernels: 90.9 us -> 87.4 us
    pallas_call x1, Pallas kernels: 90.9 us -> 83.4 us  [fused(): pl.pallas_call(functools.partial(kernel, group), out_shape=(jax.ShapeDtyp...]
    unnamed x11 -> x0, local copies, waits for them, and re-layouts: 6.27 us -> none
    pallas_call x0 -> x1, Pallas kernels: none -> 4.05 us  [deliver(): pl.pallas_call(body, grid=(steps,), out_shape=tuple((jax.ShapeDtypeStruct...]
where the time goes in v1:
time: 88.3 us; the launch traced here: 88 us
  Pallas kernels  87.4 us (99%)
    pallas_call x1, Pallas kernels, fused(): pl.pallas_call(functools.partial(kernel, group), out_shape=(jax.ShapeDtyp...  83.4 us
    pallas_call x1, Pallas kernels, deliver(): pl.pallas_call(body, grid=(steps,), out_shape=tuple((jax.ShapeDtypeStruct...  4.05 us

profile of v1, /device:TPU:0, one launch (start us, length us, event | category | flops | bytes accessed | tf_op | source)
XLA Modules:
  0.0 88.0 jit_solution(10470560324455517826)
XLA Ops:
  0.6 83.4 %shard_map.128 = (bf16[128,2048]{1,0:T(8,128)(2,1)}, bf16[128,2048]{1,0:T(8,128)(2,1)}, bf16[128,2048]{1,0:T(8,128)(2,1)}, f32[128,2048]{1,0:T(8,128)}, f32[3,2048]{1,0:T(4,128)}) custom-call(bf16[128,2048]{1,0:T(8,128)(2,1)} %query.1, bf16[128,2048]{1,0:T(8,128)(2,1)} %key.1, bf16[128,2048]{1,0:T(8,128)(2,1)} %value.1, bf16[128,2048]{1,0:T(8,128)(2,1)} %grad.1, ...), custom_call_target="tpu_custom_call" | custom-call | tf_op jit(solution)/shard_map/pallas_call | solution.py:448
  84.0 4.0 %shard_map.129 = (bf16[128,2048]{1,0:T(8,128)(2,1)}, bf16[128,2048]{1,0:T(8,128)(2,1)}, bf16[128,2048]{1,0:T(8,128)(2,1)}, f32[128,2048]{1,0:T(8,128)}, f32[3,2048]{1,0:T(4,128)}) custom-call(bf16[128,2048]{1,0:T(8,128)(2,1)} %get-tuple-element.10.refs_0_, bf16[128,2048]{1,0:T(8,128)(2,1)} %get-tuple-element.11.refs_1_, ...), custom_call_target="tpu_custom_call" | custom-call | tf_op jit(solution)/shard_map/pallas_call | solution.py:433
